TPU v7x, 512 devices: a whole 4x4x16 slice. The times are simulated.
512 devices in a mesh: copy: 32 (over y, z_lo, core), fsdp: 16 (over x, z_hi).
Axes of the slice: x: 4, y: 4, z: 16 (z_hi: 4, z_lo: 4; z = z_hi * 4 + z_lo), core: 2. Of those that a mesh axis runs over, the one named last changes fastest.
Arguments:
- hidden: bfloat16 [32, 512, 2048], P('copy', 'fsdp'), may hold values from -6 to 6, as said below
- gain: float32 [32, 2048], P('copy'), may hold values from 0.5 to 1.5
- head_weight: bfloat16 [32, 2048, 16384], P('copy', None, 'fsdp'), may hold values from -3.3766065 to 3.3766065
- targets: int32 [512], replicated, may hold values from 0 to 16383
- partner: int32 [32], replicated, may hold values from 0 to 31, each once
Outputs:
- gain_gradient: float32 [32, 2048], P('copy', 'fsdp')
- token_loss: float32 [32, 512], P('copy', 'fsdp')
Inputs may be any that keep to these rules, and one draw needn't show every extreme that they name: hidden states of order one.
All inputs are finite; a program needn't handle non-finite values.
Results may differ from a plain program's by a relative error of at most 0.013.
Values may be sent and summed in bfloat16 or wider, within the bound.
A program may use at most 64 MiB of HBM per device.

v0:
```python
import jax
import jax.numpy as jnp
from jax import lax
from jax.sharding import PartitionSpec as P

distill_weight = 0.5
stability_offset = 1e-05


def joined(value, axis, join):
    pieces = jax.tree.map(lambda part: lax.all_gather(part, axis), value)
    head = jax.tree.map(lambda part: part[0], pieces)
    tail = jax.tree.map(lambda part: part[1:], pieces)
    subtotal, _ = lax.scan(lambda subtotal, share: (join(subtotal, share), None), head, tail)
    return subtotal


def combine_totals(first_pair, second_pair):
    first_top, first_total = first_pair
    second_top, second_total = second_pair
    top = jnp.maximum(first_top, second_top)
    total = first_total * jnp.exp(first_top - top) + second_total * jnp.exp(second_top - top)
    return (top, total)


def per_device(hidden, gain, head_weight, targets, partner):
    input_rows = hidden[0]
    inverse_root_scale = gain[0]
    output_weight = head_weight[0]
    tok_rows = input_rows.shape[0]
    vocab_dev = output_weight.shape[1]
    shard_index = lax.axis_index("fsdp")
    whole = lax.all_gather(input_rows, "fsdp", axis=0, tiled=True)
    value_list = whole.astype(jnp.float32)
    centered_input = value_list * lax.rsqrt(
        jnp.mean(value_list * value_list, axis=-1, keepdims=True) + stability_offset
    )
    normalized_rows = (centered_input * inverse_root_scale[None, :]).astype(jnp.bfloat16)
    output_scores = jnp.dot(normalized_rows, output_weight, preferred_element_type=jnp.float32)
    local_top = jnp.max(output_scores, axis=-1)
    local_total = jnp.sum(jnp.exp(output_scores - local_top[:, None]), axis=-1)
    top, total = joined((local_top, local_total), "fsdp", combine_totals)
    log_probability = output_scores - top[:, None] - jnp.log(total)[:, None]
    sent = log_probability.astype(jnp.bfloat16)
    copies = lax.axis_size("copy")
    all_rows = sent.shape[0]
    pieces = sent.reshape(copies, all_rows // copies, vocab_dev)
    first = lax.all_to_all(pieces, "copy", split_axis=0, concat_axis=0, tiled=True)
    ordered = jnp.take(first, partner, axis=0)
    second = lax.all_to_all(ordered, "copy", split_axis=0, concat_axis=0, tiled=True)
    partner_logq = second.reshape(all_rows, vocab_dev).astype(jnp.float32)
    partner_q = jnp.exp(partner_logq)
    prob = jnp.exp(log_probability)
    vocab_ids = shard_index * vocab_dev + lax.broadcasted_iota(jnp.int32, (1, vocab_dev), 1)
    onehot = (targets[:, None] == vocab_ids).astype(jnp.float32)
    target_part = jnp.sum(onehot * log_probability, axis=-1)
    diverge_part = jnp.sum(partner_q * (partner_logq - log_probability), axis=-1)
    q_part = jnp.sum(partner_q, axis=-1)
    target_sum, diverge_sum, q_total = lax.psum((target_part, diverge_part, q_part), "fsdp")
    loss_all = -target_sum + distill_weight * diverge_sum
    token_loss = lax.dynamic_slice_in_dim(loss_all, shard_index * tok_rows, tok_rows, 0)
    dlogits = (prob - onehot + distill_weight * (q_total[:, None] * prob - partner_q)).astype(
        jnp.bfloat16
    )
    normalized_gradient_piece = lax.dot_general(
        dlogits, output_weight, (((1,), (1,)), ((), ())), preferred_element_type=jnp.float32
    )
    gain_gradient_piece = jnp.sum(centered_input * normalized_gradient_piece, axis=0)
    gain_gradient = lax.psum_scatter(gain_gradient_piece, "fsdp", scatter_dimension=0, tiled=True)
    return (gain_gradient[None], token_loss[None])


def solution(mesh):
    in_specs = (P("copy", "fsdp", None), P("copy", None), P("copy", None, "fsdp"), P(), P())
    out_specs = (P("copy", "fsdp"), P("copy", "fsdp"))
    return jax.shard_map(
        per_device, mesh=mesh, in_specs=in_specs, out_specs=out_specs, check_vma=False
    )
```

profile of v0, /device:TPU:24, one launch (start us, length us, event | category | flops | bytes accessed | tf_op | source)
XLA Modules:
  0.0 441.3 jit_solution(17343769877180835427)
XLA Ops:
  7.2 0.0 copy-start.3
  7.2 0.0 all-gather.7.cloned.1.call-start
  7.2 0.7 all-gather.7.cloned.1.call-update
  7.9 100.6 %all-gather.7.cloned.1.call-done = bf16[1,512,2048]{2,1,0:T(8,128)(2,1)} async-done(((bf16[1,32,2048]{2,1,0:T(8,128)(2,1)}), bf16[1,512,2048]{2,1,0:T(8,128)(2,1)}) %all-gather.7.cloned.1.call-update) | async-done | bytes 2097168 | tf_op jit(solution)/shard_map/all_gather | solution.py:33
  108.5 0.0 copy-start
  108.5 2.2 fusion.4
  110.7 0.0 copy-done.3
  110.7 0.0 copy-done
  110.7 4.7 %fusion.25 = (f32[512]{0:T(512)S(1)}, f32[512,1024]{1,0:T(8,128)S(1)}) fusion(bf16[1,2048,1024]{2,1,0:T(8,128)(2,1)} %param.9, bf16[1,512,2048]{2,1,0:T(8,128)(2,1)S(1)} %copy-done, f32[2048]{0:T(1024)S(1)} %bitcast.66, f32[512]{0:T(512)S(1)} %add_rsqrt_fusion), kind=kOutput, calls=%fused_computation.46 | convolution fusion | flops 2152201728 | bytes 8400896 | tf_op jit(solution)/shard_map/dot_general | solution.py:39
  115.4 0.5 exponential_reduce_fusion
  115.9 50.8 %all-gather.4 = f32[16,1,512]{2,1,0:T(1,128)S(1)} all-gather(f32[1,1,512]{2,1,0:T(1,128)S(1)} %bitcast.65), channel_id=4, replica_groups=mesh['copy'=32,'fsdp'=16] {'fsdp'}, dimensions={0}, use_global_device_ids=true | all-gather | bytes 34816 | tf_op jit(solution)/shard_map/all_gather | solution.py:11
  166.7 45.7 %all-gather.3 = f32[16,1,512]{2,1,0:T(1,128)S(1)} all-gather(f32[1,1,512]{2,1,0:T(1,128)S(1)} %bitcast.64), channel_id=3, replica_groups=mesh['copy'=32,'fsdp'=16] {'fsdp'}, dimensions={0}, use_global_device_ids=true | all-gather | bytes 34816 | tf_op jit(solution)/shard_map/all_gather | solution.py:11
  212.4 0.8 while.12
  213.2 0.0 copy-start.4
  213.3 1.2 fusion.24
  214.5 7.7 %all-to-all-start = ((bf16[32,16,1024]{2,1,0:T(8,128)(2,1)}), bf16[32,16,1024]{2,1,0:T(8,128)(2,1)}, u32[]{:S(2)}, u32[]{:S(2)}) async-start(bf16[32,16,1024]{2,1,0:T(8,128)(2,1)} %bitcast.10), calls=%async_computation | async-start | bytes 2097152 | tf_op jit(solution)/shard_map/all_to_all | solution.py:48
  222.2 0.0 copy-done.4
  222.2 25.7 %all-to-all-done = bf16[32,16,1024]{2,1,0:T(8,128)(2,1)} async-done(((bf16[32,16,1024]{2,1,0:T(8,128)(2,1)}), bf16[32,16,1024]{2,1,0:T(8,128)(2,1)}, u32[]{:S(2)}, u32[]{:S(2)}) %all-to-all-start) | async-done | bytes 1048608 | tf_op jit(solution)/shard_map/all_to_all | solution.py:48
  248.0 1.8 gather_fusion
  249.8 1.1 broadcast_select_fusion
  250.9 0.0 copy-start.2
  250.9 6.3 %all-to-all-start.1 = ((bf16[32,16,1024]{2,1,0:T(8,128)(2,1)}), bf16[32,16,1024]{2,1,0:T(8,128)(2,1)S(1)}, u32[]{:S(2)}, u32[]{:S(2)}) async-start(bf16[32,16,1024]{2,1,0:T(8,128)(2,1)} %broadcast_select_fusion), calls=%async_computation.1 | async-start | bytes 2097152 | tf_op jit(solution)/shard_map/all_to_all | solution.py:50
  257.3 1.3 dynamic-slice
  259.2 23.8 %all-to-all-done.1 = bf16[32,16,1024]{2,1,0:T(8,128)(2,1)S(1)} async-done(((bf16[32,16,1024]{2,1,0:T(8,128)(2,1)}), bf16[32,16,1024]{2,1,0:T(8,128)(2,1)S(1)}, u32[]{:S(2)}, u32[]{:S(2)}) %all-to-all-start.1) | async-done | bytes 1048608 | tf_op jit(solution)/shard_map/all_to_all | solution.py:50
  283.0 0.3 fusion.18
  283.3 0.1 reduce_sum.59
  283.4 49.1 %psum.21 = f32[512]{0:T(512)S(1)} all-reduce(f32[512]{0:T(512)S(1)} %reduce_sum.59), channel_id=1, replica_groups=mesh['copy'=32,'fsdp'=16] {'fsdp'}, use_global_device_ids=true, to_apply=%region_6.7 | all-reduce | flops 512 | bytes 4096 | tf_op jit(solution)/shard_map/psum | solution.py:59
  332.5 0.0 copy-done.2
  332.5 0.0 copy-start.1
  332.5 2.0 fusion.12
  334.6 0.0 copy-done.1
  334.6 4.6 %fusion.3 = f32[2048]{0:T(1024)S(1)} fusion(bf16[1,512,2048]{2,1,0:T(8,128)(2,1)S(1)} %copy-done.1, f32[512]{0:T(512)S(1)} %add_rsqrt_fusion, bf16[512,1024]{1,0:T(8,128)(2,1)S(1)} %get-tuple-element.51, bf16[1,2048,1024]{2,1,0:T(8,128)(2,1)} %param.9), kind=kOutput, calls=%fused_computation.9 | convolution fusion | flops 2151675904 | bytes 7350272 | tf_op jit(solution)/shard_map/dot_general | solution.py:65
  339.2 94.1 %all-reduce.1 = (f32[2048]{0:T(1024)S(1)}, f32[512]{0:T(512)S(1)}, f32[512]{0:T(512)S(1)}) all-reduce(f32[2048]{0:T(1024)S(1)} %fusion.3, f32[512]{0:T(512)S(1)} %get-tuple-element.33, f32[512]{0:T(512)S(1)} %get-tuple-element.32), channel_id=5, replica_groups=mesh['copy'=32,'fsdp'=16] {'fsdp'}, use_global_device_ids=true, to_apply=%region_8.9.clone | all-reduce | flops 3072 | bytes 24576
  433.3 0.6 dynamic-slice_bitcast_fusion.1
  433.9 0.6 dynamic-slice_bitcast_fusion
  (43 shorter events, 0.5 us)
Async XLA Ops:
  7.2 103.5 %copy-start.3 = (f32[1,2048]{1,0:T(1,128)S(1)}, f32[1,2048]{1,0:T(1,128)}, u32[]{:S(2)}) copy-start(f32[1,2048]{1,0:T(1,128)} %param.8) | copy-start | bytes 24580
  7.2 101.3 %all-gather.7.cloned.1.call-start = ((), (), s32[]{:S(2)}) async-start(), calls=%async_computation.2 | async-start | bytes 2228224 | tf_op jit(solution)/shard_map/all_gather | solution.py:33
  108.5 2.2 copy-start
  213.2 8.9 %copy-start.4 = (s32[32]{0:T(128)S(1)}, s32[32]{0:T(128)}, u32[]{:S(2)}) copy-start(s32[32]{0:T(128)} %param.11) | copy-start | bytes 388
  214.5 33.4 %all-to-all-start = ((bf16[32,16,1024]{2,1,0:T(8,128)(2,1)}), bf16[32,16,1024]{2,1,0:T(8,128)(2,1)}, u32[]{:S(2)}, u32[]{:S(2)}) async-start(bf16[32,16,1024]{2,1,0:T(8,128)(2,1)} %bitcast.10), calls=%async_computation | async-start | bytes 2097152 | tf_op jit(solution)/shard_map/all_to_all | solution.py:48
  250.9 81.6 %copy-start.2 = (s32[512]{0:T(512)S(1)}, s32[512]{0:T(512)}, u32[]{:S(2)}) copy-start(s32[512]{0:T(512)} %param.10) | copy-start | bytes 6148
  250.9 32.0 %all-to-all-start.1 = ((bf16[32,16,1024]{2,1,0:T(8,128)(2,1)}), bf16[32,16,1024]{2,1,0:T(8,128)(2,1)S(1)}, u32[]{:S(2)}, u32[]{:S(2)}) async-start(bf16[32,16,1024]{2,1,0:T(8,128)(2,1)} %broadcast_select_fusion), calls=%async_computation.1 | async-start | bytes 2097152 | tf_op jit(solution)/shard_map/all_to_all | solution.py:50
  332.5 2.0 copy-start.1
Sparse Core Ops, SparseCore 0:
  11.0 97.3 all-gather.6
where the time goes:
time: 442 us; the launch traced here: 441 us
  blocking collectives  240 us (54%)
  waiting for transfers between devices  151 us (34%)
  between operations  14.8 us (3%)
  starting transfers between devices  14 us (3%)
  matrix products  9.27 us (2%)
  other arithmetic  7.81 us (2%)
  local copies, waits for them, and re-layouts  4.57 us (1%)
    all_gather x1, waiting for transfers between devices, per_device(): whole = lax.all_gather(input_rows, 'fsdp', axis=0, tiled=True)  101 us
    all_gather x2, blocking collectives, joined(): pieces = jax.tree.map(lambda part: lax.all_gather(part, axis), value)  96.5 us
    unnamed x1, blocking collectives  94.1 us
    psum x1, blocking collectives, per_device(): lax.psum((target_part, diverge_part, q_part), 'fsdp')  49.1 us
    all_to_all x1, waiting for transfers between devices, per_device(): lax.all_to_all(pieces, 'copy', split_axis=0, concat_axis=0, tiled=True)  25.7 us
    all_to_all x1, waiting for transfers between devices, per_device(): lax.all_to_all(ordered, 'copy', split_axis=0, concat_axis=0, tiled=True)  23.8 us
  transfers between devices with their start and end apart: 3, of which 3 were waited for; matrix products, arithmetic and copies ran while one was open for 0% of the time, Pallas kernels for 0%

commit v1 on v0

v1 whole, which is shorter than its diff:
```python
import functools

import jax
import jax.numpy as jnp
from jax import lax
from jax.experimental import pallas as pl
from jax.experimental.pallas import tpu as pltpu
from jax.sharding import PartitionSpec as P

MESH = pl.DeviceIdType.MESH
F32, BF16 = jnp.float32, jnp.bfloat16
WEIGHT = 0.5
OFFSET = 1e-05
RING = 4
ROWS = 16
HALVES = 2
BLOCK = 256
LANES = 128


def column_of(row):
    return jnp.broadcast_to(row, (LANES, LANES)).T


def kernel(
    copies, shards, hidden, gain, w_hbm, targets, partner, gg_out, tl_out,
    w, hid, xhat, normed, logp, dlog, lse_col, q_col, t_col, loss_col, gacc,
    stat_src, stat_buf, qs_src, qs_buf, qc_src, qc_buf, fin_src, fin_buf,
    stage1, buf1_first, buf1_second, stage2, buf2,
    w_sem, z_send, z_recv, x_send, x_recv, s_send, s_recv, qs_send, qs_recv, qc_send, qc_recv,
    f_send, f_recv, p1_send, p1_recv, p2_send, p2_recv,
):
    buf1 = (buf1_first, buf1_second)
    me_c, me_f = lax.axis_index("copy"), lax.axis_index("fsdp")
    me_x, me_z = me_f // RING, lax.rem(me_f, RING)
    vocab = w.shape[1]
    depth = w.shape[0]
    half_tokens = shards * ROWS
    piece_rows, piece_cols = stage1.shape[2], stage1.shape[3]
    splits = vocab // piece_cols

    load_w = pltpu.make_async_copy(w_hbm, w, w_sem)
    load_w.start()

    barrier = pltpu.get_barrier_semaphore()

    def greet_copy(k, carry):
        pl.semaphore_signal(barrier, inc=1, device_id=(lax.rem(me_c + k, copies), me_f), device_id_type=MESH)
        return carry

    def greet_shard(k, carry):
        pl.semaphore_signal(barrier, inc=1, device_id=(me_c, lax.rem(me_f + k, shards)), device_id_type=MESH)
        return carry

    lax.fori_loop(1, shards, greet_shard, 0)
    lax.fori_loop(1, copies, greet_copy, 0)
    for half in range(HALVES):
        hid[me_f, half] = hidden[half * ROWS : (half + 1) * ROWS, :]
    pl.semaphore_wait(barrier, copies + shards - 2)

    def shard_of(dx, dz):
        return lax.rem(me_x + dx + RING, RING) * RING + lax.rem(me_z + dz + RING, RING)

    def hop(which, half, to, send, recv):
        return pltpu.make_async_remote_copy(
            src_ref=hid.at[which, half], dst_ref=hid.at[which, half], send_sem=send, recv_sem=recv,
            device_id=(me_c, to), device_id_type=MESH,
        )

    def z_copy(half, slot):
        onward = 1 - 2 * half
        dz, to = ((0, onward), (0, -onward), (-onward, onward))[slot]
        return hop(shard_of(0, dz), half, shard_of(0, to), z_send.at[half * 3 + slot], z_recv.at[half * 3 + slot])

    def z_offset(half, slot):
        onward = 1 - 2 * half
        return (-onward, onward, -2 * onward)[slot]

    def x_copy(half, order, slot):
        onward = 1 - 2 * half
        dz = 0 if order == 0 else z_offset(half, order - 1)
        dx, to = ((0, onward), (0, -onward), (-onward, onward))[slot]
        at = (half * RING + order) * 3 + slot
        return hop(shard_of(dx, dz), half, shard_of(to, 0), x_send.at[at], x_recv.at[at])

    def spread(half, order):
        x_copy(half, order, 0).start()
        x_copy(half, order, 1).start()

    def pass_on(half, order):
        x_copy(half, order, 0).wait_recv()
        x_copy(half, order, 2).start()

    def gather_start(half):
        z_copy(half, 0).start()
        z_copy(half, 1).start()
        spread(half, 0)

    def gather_first(half):
        pass_on(half, 0)
        z_copy(half, 0).wait_recv()
        z_copy(half, 2).start()
        spread(half, 1)
        z_copy(half, 1).wait_recv()
        spread(half, 2)

    def gather_second(half):
        pass_on(half, 1)
        pass_on(half, 2)
        z_copy(half, 2).wait_recv()
        spread(half, 3)
        pass_on(half, 3)

    def gather_end(half):
        for order in range(RING):
            x_copy(half, order, 1).wait_recv()
            x_copy(half, order, 2).wait_recv()

    def to_all(axis, src_of, buf, send, recv):
        size = copies if axis == "copy" else shards

        def step(k, carry):
            if axis == "copy":
                peer = lax.rem(me_c + k, size)
                device = (peer, me_f)
            else:
                peer = lax.rem(me_f + k, size)
                device = (me_c, peer)
            pltpu.make_async_remote_copy(
                src_ref=src_of(peer, k), dst_ref=buf.at[k], send_sem=send, recv_sem=recv,
                device_id=device, device_id_type=MESH,
            ).start()
            return carry

        lax.fori_loop(1, size, step, 0)

    def wait_all(buf, sem):
        rest = buf.at[pl.ds(1, buf.shape[0] - 1)]
        pltpu.make_async_copy(rest, rest, sem).wait()

    def normalise(half):
        def step(s, carry):
            rows = pl.ds(pl.multiple_of(half * half_tokens + s * ROWS, ROWS), ROWS)
            value = hid[s, half].astype(F32)
            scale = lax.rsqrt(jnp.mean(value * value, axis=-1, keepdims=True) + OFFSET)
            unit = value * scale
            xhat[rows, :] = unit
            normed[rows, :] = (unit * gain[...]).astype(BF16)
            return carry

        lax.fori_loop(0, shards, step, 0)

    def head(half):
        rows = pl.ds(half * half_tokens, half_tokens)

        def step(b, carry):
            cols = pl.ds(pl.multiple_of(b * BLOCK, BLOCK), BLOCK)
            logp[rows, cols] = jnp.dot(normed[rows, :], w[:, cols], preferred_element_type=F32)
            return carry

        lax.fori_loop(0, vocab // BLOCK, step, 0)

        def total(s, carry):
            at = pl.ds(pl.multiple_of(half * half_tokens + s * ROWS, ROWS), ROWS)
            value = logp[at, :]
            top = jnp.max(value, axis=-1, keepdims=True)
            local = top + jnp.log(jnp.sum(jnp.exp(value - top), axis=-1, keepdims=True))
            lse_col[at, :] = jnp.broadcast_to(local, (ROWS, LANES))
            return carry

        lax.fori_loop(0, shards, total, 0)
        for part in range(half_tokens // LANES):
            at = pl.ds(half * half_tokens + part * LANES, LANES)
            stat_src[half, part : part + 1, :] = lse_col[at, :].T[0:1, :]
        stat_buf[half, 0] = stat_src[half]
        to_all("fsdp", lambda peer, k: stat_src.at[half], stat_buf.at[half], s_send.at[half], s_recv.at[half])

    def log_probability(half):
        wait_all(stat_buf.at[half], s_recv.at[half])
        parts = stat_buf[half]
        top = jnp.max(parts, axis=0)
        lse = top + jnp.log(jnp.sum(jnp.exp(parts - top[None]), axis=0))
        for part in range(half_tokens // LANES):
            at = pl.ds(half * half_tokens + part * LANES, LANES)
            lse_col[at, :] = column_of(lse[part : part + 1, :])

        def step(s, carry):
            at = pl.ds(pl.multiple_of(half * half_tokens + s * ROWS, ROWS), ROWS)
            value = logp[at, :] - lse_col[at, 0:1]
            logp[at, :] = value
            rounded = value.astype(BF16)
            first = (s * ROWS) // piece_rows * splits
            inner = pl.ds(pl.multiple_of(lax.rem(s * ROWS, piece_rows), ROWS), ROWS)
            for split in range(splits):
                stage1[half, first + split, inner, :] = rounded[:, split * piece_cols : (split + 1) * piece_cols]
            part = jnp.sum(jnp.exp(rounded.astype(F32)), axis=-1, keepdims=True)
            q_col[at, :] = jnp.broadcast_to(part, (ROWS, LANES))
            return carry

        lax.fori_loop(0, shards, step, 0)

    def exchange_first(half):
        to_all("copy", lambda peer, k: stage1.at[half, peer], buf1[half], p1_send.at[half], p1_recv.at[half])
        buf1[half][0] = stage1[half, me_c]

    def exchange_second(half):
        wait_all(buf1[half], p1_recv.at[half])

        def pick(j, carry):
            source = partner[lax.rem(me_c + j, copies)]
            stage2[half, j] = buf1[half][lax.rem(me_c - source + copies, copies)]
            return carry

        lax.fori_loop(0, copies, pick, 0)
        to_all("copy", lambda peer, k: stage2.at[half, k], buf2.at[half], p2_send.at[half], p2_recv.at[half])
        buf2[half, 0] = stage2[half, 0]

    def totals_first():
        for part in range(HALVES * half_tokens // LANES):
            qs_src[part : part + 1, :] = q_col[part * LANES : (part + 1) * LANES, :].T[0:1, :]
        qs_buf[0] = qs_src[...]
        to_all("fsdp", lambda peer, k: qs_src, qs_buf, qs_send.at[0], qs_recv.at[0])

    def totals_second():
        wait_all(qs_buf, qs_recv.at[0])
        qc_src[...] = jnp.sum(qs_buf[...], axis=0)
        qc_buf[0] = qc_src[...]
        to_all("copy", lambda peer, k: qc_src, qc_buf, qc_send.at[0], qc_recv.at[0])

    def totals_third():
        wait_all(qc_buf, qc_recv.at[0])
        mine = qc_buf[lax.rem(me_c - partner[me_c] + copies, copies)]
        for part in range(HALVES * half_tokens // LANES):
            q_col[part * LANES : (part + 1) * LANES, :] = column_of(mine[part : part + 1, :])

    def backward(half):
        wait_all(buf2.at[half], p2_recv.at[half])
        base = me_f * vocab

        def step(s, carry):
            at = pl.ds(pl.multiple_of(half * half_tokens + s * ROWS, ROWS), ROWS)
            here = pl.ds(pl.multiple_of(s * ROWS, ROWS), ROWS)
            token = pl.ds(pl.multiple_of(s * (HALVES * ROWS) + half * ROWS, ROWS), ROWS)
            first = (s * ROWS) // piece_rows * splits
            inner = pl.ds(pl.multiple_of(lax.rem(s * ROWS, piece_rows), ROWS), ROWS)
            q_total = q_col[at, 0:1]
            target = t_col[token, 0:1]
            loss = jnp.zeros((ROWS, 1), F32)
            for split in range(splits):
                cols = slice(split * piece_cols, (split + 1) * piece_cols)
                slot = lax.rem(me_c - (first + split) + copies, copies)
                logq = buf2[half, slot, inner, :].astype(F32)
                q = jnp.exp(logq)
                value = logp[at, cols]
                prob = jnp.exp(value)
                ids = base + split * piece_cols + lax.broadcasted_iota(jnp.int32, (ROWS, piece_cols), 1)
                hot = ids == target
                term = WEIGHT * (q * (logq - value)) - jnp.where(hot, value, 0.0)
                loss = loss + jnp.sum(term, axis=-1, keepdims=True)
                slope = prob - jnp.where(hot, 1.0, 0.0) + WEIGHT * (q_total * prob - q)
                dlog[here, cols] = slope.astype(BF16)
            loss_col[token, :] = jnp.broadcast_to(loss, (ROWS, LANES))
            return carry

        lax.fori_loop(0, shards, step, 0)
        rows = pl.ds(half * half_tokens, half_tokens)

        def product(b, carry):
            at = pl.ds(pl.multiple_of(b * BLOCK, BLOCK), BLOCK)
            piece = lax.dot_general(
                dlog[...], w[at, :], (((1,), (1,)), ((), ())), preferred_element_type=F32
            )
            part = jnp.sum(xhat[rows, at] * piece, axis=0, keepdims=True)
            if half == 0:
                gacc[:, at] = part
            else:
                gacc[:, at] = gacc[:, at] + part
            return carry

        lax.fori_loop(0, depth // BLOCK, product, 0)

    gather_start(0)
    stat_src[...] = jnp.zeros_like(stat_src)
    qs_src[...] = jnp.zeros_like(qs_src)
    fin_src[...] = jnp.zeros_like(fin_src)
    for part in range(HALVES * half_tokens // LANES):
        at = pl.ds(part * LANES, LANES)
        row = targets[part : part + 1, :]
        t_col[at, :] = column_of(row)
    gather_first(0)
    z_copy(1, 0).start()
    gather_second(0)
    z_copy(1, 1).start()
    spread(1, 0)
    gather_end(0)
    normalise(0)
    load_w.wait()
    head(0)
    gather_first(1)
    log_probability(0)
    exchange_first(0)
    gather_second(1)
    gather_end(1)
    normalise(1)
    head(1)
    log_probability(1)
    exchange_first(1)
    totals_first()
    exchange_second(0)
    totals_second()
    exchange_second(1)
    totals_third()
    backward(0)
    backward(1)

    per_row = LANES // (HALVES * ROWS)
    for part in range(shards // per_row):
        row = loss_col[part * LANES : (part + 1) * LANES, :].T[0:1, :]
        for j in range(part * per_row, (part + 1) * per_row):
            fin_src[j, 0:1, :] = gacc[:, j * LANES : (j + 1) * LANES]
            fin_src[j, 1:2, :] = row
    to_all("fsdp", lambda peer, k: fin_src.at[peer], fin_buf, f_send.at[0], f_recv.at[0])
    fin_buf[0] = fin_src[me_f]

    for half in range(HALVES):
        for slot in range(3):
            z_copy(half, slot).wait_send()
            for order in range(RING):
                x_copy(half, order, slot).wait_send()
        wait_all(stat_buf.at[half], s_send.at[half])
        wait_all(buf1[half], p1_send.at[half])
        wait_all(buf2.at[half], p2_send.at[half])
    wait_all(qs_buf, qs_send.at[0])
    wait_all(qc_buf, qc_send.at[0])
    wait_all(fin_buf, f_send.at[0])

    wait_all(fin_buf, f_recv.at[0])
    whole = jnp.sum(fin_buf[...], axis=0)
    gg_out[...] = whole[0:1, :]
    wide = HALVES * ROWS
    row = whole[1:2, :]
    result = row[:, 0:wide]
    for k in range(1, per_row):
        result = jnp.where(lax.rem(me_f, per_row) == k, row[:, k * wide : (k + 1) * wide], result)
    tl_out[...] = result


def per_device(copies, shards, hidden, gain, head_weight, targets, partner):
    mine, depth = hidden.shape[1], hidden.shape[2]
    vocab = head_weight.shape[2]
    tokens = mine * shards
    half_tokens = tokens // HALVES
    groups = min(half_tokens // ROWS, copies)
    piece = (half_tokens // groups, vocab // (copies // groups))
    vmem = pl.BlockSpec(memory_space=pltpu.VMEM)
    dma = pltpu.SemaphoreType.DMA
    return pl.pallas_call(
        functools.partial(kernel, copies, shards),
        out_shape=(
            jax.ShapeDtypeStruct((1, depth // shards), F32),
            jax.ShapeDtypeStruct((1, mine), F32),
        ),
        in_specs=[vmem, vmem, pl.BlockSpec(memory_space=pl.ANY), vmem, pl.BlockSpec(memory_space=pltpu.SMEM)],
        out_specs=(vmem, vmem),
        scratch_shapes=[
            pltpu.VMEM((depth, vocab), BF16),
            pltpu.VMEM((shards, HALVES, ROWS, depth), BF16),
            pltpu.VMEM((tokens, depth), F32),
            pltpu.VMEM((tokens, depth), BF16),
            pltpu.VMEM((tokens, vocab), F32),
            pltpu.VMEM((half_tokens, vocab), BF16),
            pltpu.VMEM((tokens, LANES), F32),
            pltpu.VMEM((tokens, LANES), F32),
            pltpu.VMEM((tokens, LANES), jnp.int32),
            pltpu.VMEM((tokens, LANES), F32),
            pltpu.VMEM((1, depth), F32),
            pltpu.VMEM((HALVES, 8, LANES), F32),
            pltpu.VMEM((HALVES, shards, 8, LANES), F32),
            pltpu.VMEM((8, LANES), F32),
            pltpu.VMEM((shards, 8, LANES), F32),
            pltpu.VMEM((8, LANES), F32),
            pltpu.VMEM((copies, 8, LANES), F32),
            pltpu.VMEM((shards, 8, LANES), F32),
            pltpu.VMEM((shards, 8, LANES), F32),
        ]
        + [
            pltpu.VMEM((HALVES, copies) + piece, BF16),
            pltpu.VMEM((copies,) + piece, BF16),
            pltpu.VMEM((copies,) + piece, BF16),
            pltpu.VMEM((HALVES, copies) + piece, BF16),
            pltpu.VMEM((HALVES, copies) + piece, BF16),
        ]
        + [
            dma,
            dma((HALVES * 3,)),
            dma((HALVES * 3,)),
            dma((HALVES * RING * 3,)),
            dma((HALVES * RING * 3,)),
            dma((HALVES,)),
            dma((HALVES,)),
        ]
        + [dma((1,))] * 6
        + [dma((HALVES,))] * 4,
        compiler_params=pltpu.CompilerParams(
            collective_id=0, has_side_effects=True, vmem_limit_bytes=48 * 1024 * 1024
        ),
        cost_estimate=pl.CostEstimate(
            flops=4 * tokens * depth * vocab,
            bytes_accessed=2 * depth * vocab,
            transcendentals=4 * tokens * vocab,
        ),
    )(hidden[0], gain, head_weight[0], targets.reshape(-1, LANES), partner)


def solution(mesh):
    in_specs = (P("copy", "fsdp", None), P("copy", None), P("copy", None, "fsdp"), P(), P())
    out_specs = (P("copy", "fsdp"), P("copy", "fsdp"))
    return jax.shard_map(
        functools.partial(per_device, mesh.shape["copy"], mesh.shape["fsdp"]),
        mesh=mesh, in_specs=in_specs, out_specs=out_specs, check_vma=False,
    )
```

time: 442 us -> 147 us (0.33)
  the two profiles are of different devices: /device:TPU:24 before, /device:TPU:1 now
where the time goes in v1:
time: 147 us
  Pallas kernels  140 us (95%)
  local copies, waits for them, and re-layouts  6.14 us (4%)
    pallas_call x1, Pallas kernels, per_device(): pl.pallas_call(functools.partial(kernel, copies, shards), out_shape=(jax....  140 us
    unnamed x12, local copies, waits for them, and re-layouts  6.14 us

profile of v1, /device:TPU:1, one launch (start us, length us, event | category | flops | bytes accessed | tf_op | source)
XLA Modules:
  0.0 146.9 jit_solution(5789325837744002520)
XLA Ops:
  0.6 0.0 copy-start
  0.6 2.2 %copy-done = bf16[1,2048,1024]{2,1,0:T(8,128)(2,1)S(1)} copy-done((bf16[1,2048,1024]{2,1,0:T(8,128)(2,1)S(1)}, bf16[1,2048,1024]{2,1,0:T(8,128)(2,1)}, u32[]{:S(2)}) %copy-start) | copy-done | bytes 4194328
  2.8 0.0 copy-start.1
  2.8 0.9 copy-done.1
  3.7 0.0 copy-start.2
  3.7 0.7 copy-done.2
  4.4 0.0 copy-start.3
  4.4 0.7 copy-done.3
  5.1 0.0 copy-start.4
  5.1 0.7 copy-done.4
  5.8 140.1 %shard_map.68 = (f32[1,128]{1,0:T(1,128)S(1)}, f32[1,32]{1,0:T(1,128)S(1)}) custom-call(bf16[32,2048]{1,0:T(8,128)(2,1)S(1)} %bitcast.4, f32[1,2048]{1,0:T(1,128)S(1)} %copy-done.2, bf16[2048,1024]{1,0:T(8,128)(2,1)S(1)} %bitcast.3, s32[4,128]{1,0:T(4,128)S(1)} %bitcast.5, s32[32]{0:T(128)S(1)} %copy-done.4), custom_call_target="tpu_custom_call" | custom-call | flops 4294967296 | bytes 4194304 | tf_op jit(solution)/shard_map/pallas_call | solution.py:357
  145.8 0.5 copy.9
  146.4 0.5 copy.10
Async XLA Ops:
  0.6 2.2 %copy-start = (bf16[1,2048,1024]{2,1,0:T(8,128)(2,1)S(1)}, bf16[1,2048,1024]{2,1,0:T(8,128)(2,1)}, u32[]{:S(2)}) copy-start(bf16[1,2048,1024]{2,1,0:T(8,128)(2,1)} %param.7) | copy-start | bytes 12582916
  2.8 0.9 copy-start.1
  3.7 0.7 copy-start.2
  4.4 0.7 copy-start.3
  5.1 0.7 copy-start.4

commit v2 on v0

v2 whole, which is shorter than its diff:
```python
import functools

import jax
import jax.numpy as jnp
from jax import lax
from jax.experimental import pallas as pl
from jax.experimental.pallas import tpu as pltpu
from jax.sharding import PartitionSpec as P

MESH = pl.DeviceIdType.MESH
F32, BF16 = jnp.float32, jnp.bfloat16
WEIGHT = 0.5
OFFSET = 1e-05
RING = 4
CHUNKS = RING
ROWS = 16
BLOCK = 256
LANES = 128


def column_of(row):
    return jnp.broadcast_to(row, (LANES, LANES)).T


def kernel(
    copies, shards, hidden_in, gain_in, w_in, targets_in, partner_in, gg_out, tl_out,
    w, hid, gain, targets, partner, xhat, normed, logits, dlog, stat_col, t_col, loss_col, turned, gacc,
    sx_src, sx_buf, sz_src, sz_buf, cq_src, cq_buf, fin_src, fin_buf,
    stage1, buf1_0, buf1_1, buf1_2, buf1_3, stage2, buf2,
    in_sem, z_send, z_recv, x_send, x_recv, sx_send, sx_recv, sz_send, sz_recv, cq_send, cq_recv, f_send, f_recv,
    p1_send, p1_recv, p2_send, p2_recv,
):
    buf1 = (buf1_0, buf1_1, buf1_2, buf1_3)
    me_c, me_f = lax.axis_index("copy"), lax.axis_index("fsdp")
    me_x, me_z = me_f // RING, lax.rem(me_f, RING)
    depth, vocab = w.shape
    share = hid.shape[1]
    half_share = share // 2
    tokens = share * RING
    piece_rows, piece_cols = stage1.shape[2], stage1.shape[3]
    splits = vocab // piece_cols

    loads = [
        pltpu.make_async_copy(source, target, in_sem.at[i])
        for i, (source, target) in enumerate(
            ((hidden_in, hid.at[me_f]), (partner_in, partner), (targets_in, targets), (gain_in, gain), (w_in, w))
        )
    ]
    for load in loads:
        load.start()

    barrier = pltpu.get_barrier_semaphore()

    def greet_copy(k, carry):
        pl.semaphore_signal(barrier, inc=1, device_id=(lax.rem(me_c + k, copies), me_f), device_id_type=MESH)
        return carry

    def greet_shard(k, carry):
        pl.semaphore_signal(barrier, inc=1, device_id=(me_c, lax.rem(me_f + k, shards)), device_id_type=MESH)
        return carry

    lax.fori_loop(1, shards, greet_shard, 0)
    lax.fori_loop(1, copies, greet_copy, 0)
    sx_src[...] = jnp.zeros_like(sx_src)
    fin_src[...] = jnp.zeros_like(fin_src)
    turned[...] = jnp.zeros_like(turned)
    for load in loads[:3]:
        load.wait()
    for part in range(CHUNKS * tokens // LANES):
        t_col[part * LANES : (part + 1) * LANES, :] = column_of(targets[part : part + 1, :])
    pl.semaphore_wait(barrier, copies + shards - 2)

    def shard_of(dx, dz):
        return lax.rem(me_x + dx + RING, RING) * RING + lax.rem(me_z + dz + RING, RING)

    def hop(which, half, to, send, recv):
        rows = pl.ds(half * half_share, half_share)
        return pltpu.make_async_remote_copy(
            src_ref=hid.at[which, rows], dst_ref=hid.at[which, rows], send_sem=send, recv_sem=recv,
            device_id=(me_c, to), device_id_type=MESH,
        )

    def z_copy(half, slot):
        onward = 1 - 2 * half
        dz, to = ((0, onward), (0, -onward), (-onward, onward))[slot]
        at = half * 3 + slot
        return hop(shard_of(0, dz), half, shard_of(0, to), z_send.at[at], z_recv.at[at])

    CHUNK_Z = (0, -1, 1, 2)

    def x_copy(half, chunk, slot):
        onward = 1 - 2 * half
        dx, to = ((0, onward), (0, -onward), (-onward, onward))[slot]
        at = (half * CHUNKS + chunk) * 3 + slot
        return hop(shard_of(dx, CHUNK_Z[chunk]), half, shard_of(to, 0), x_send.at[at], x_recv.at[at])

    def spread(half, chunk):
        x_copy(half, chunk, 0).start()
        x_copy(half, chunk, 1).start()

    def pass_on(chunk):
        for half in (0, 1):
            x_copy(half, chunk, 0).wait_recv()
            x_copy(half, chunk, 2).start()

    def gather_end(chunk):
        for half in (0, 1):
            x_copy(half, chunk, 1).wait_recv()
            x_copy(half, chunk, 2).wait_recv()

    def to_all(axis, src_of, buf, send, recv):
        size = buf.shape[0]

        def step(k, carry):
            if axis == "copy":
                peer = lax.rem(me_c + k, size)
                device = (peer, me_f)
            elif axis == "fsdp":
                peer = lax.rem(me_f + k, size)
                device = (me_c, peer)
            elif axis == "x":
                peer = shard_of(k, 0)
                device = (me_c, peer)
            else:
                peer = shard_of(0, k)
                device = (me_c, peer)
            pltpu.make_async_remote_copy(
                src_ref=src_of(peer, k), dst_ref=buf.at[k], send_sem=send, recv_sem=recv,
                device_id=device, device_id_type=MESH,
            ).start()
            return carry

        lax.fori_loop(1, size, step, 0)

    def wait_all(buf, sem):
        rest = buf.at[pl.ds(1, buf.shape[0] - 1)]
        pltpu.make_async_copy(rest, rest, sem).wait()

    def chunk_z(chunk):
        return lax.rem(me_z + CHUNK_Z[chunk] + RING, RING)

    def rows_of(z, g):
        return pl.ds(pl.multiple_of(z * tokens + g * ROWS, ROWS), ROWS)

    def place(g):
        first = (g * ROWS) // piece_rows * splits
        return first, pl.ds(pl.multiple_of(lax.rem(g * ROWS, piece_rows), ROWS), ROWS)

    groups = tokens // ROWS
    lane = lax.broadcasted_iota(jnp.int32, (ROWS, LANES), 1)

    def forward(chunk):
        z = chunk_z(chunk)

        def normalise(g, carry):
            at = rows_of(z, g)
            inside = pl.ds(pl.multiple_of(lax.rem(g * ROWS, share), ROWS), ROWS)
            value = hid[(g * ROWS) // share * RING + z, inside, :].astype(F32)
            scale = lax.rsqrt(jnp.mean(value * value, axis=-1, keepdims=True) + OFFSET)
            unit = value * scale
            xhat[at, :] = unit
            normed[at, :] = (unit * gain[...]).astype(BF16)
            return carry

        lax.fori_loop(0, groups, normalise, 0, unroll=2)
        rows = pl.ds(pl.multiple_of(z * tokens, tokens), tokens)

        def product(b, carry):
            cols = pl.ds(pl.multiple_of(b * BLOCK, BLOCK), BLOCK)
            logits[rows, cols] = jnp.dot(normed[rows, :], w[:, cols], preferred_element_type=F32)
            return carry

        lax.fori_loop(0, vocab // BLOCK, product, 0)

        def rounded(g, carry):
            at = rows_of(z, g)
            value = logits[at, :]
            top = jnp.max(value, axis=-1, keepdims=True)
            stat_col[at, :] = jnp.broadcast_to(top, (ROWS, LANES))
            short = (value - top).astype(BF16)
            first, inner = place(g)
            for split in range(splits):
                stage1[chunk, first + split, inner, :] = short[:, split * piece_cols : (split + 1) * piece_cols]
            return carry

        lax.fori_loop(0, groups, rounded, 0, unroll=2)
        to_all("copy", lambda peer, k: stage1.at[chunk, peer], buf1[chunk], p1_send.at[chunk], p1_recv.at[chunk])
        buf1[chunk][0] = stage1[chunk, me_c]

    def sums(chunk):
        z = chunk_z(chunk)

        def step(g, carry):
            at = rows_of(z, g)
            top = stat_col[at, :]
            total = jnp.sum(jnp.exp(logits[at, :] - top[:, 0:1]), axis=-1, keepdims=True)
            first, inner = place(g)
            q_total = jnp.zeros((ROWS, 1), F32)
            for split in range(splits):
                short = stage1[chunk, first + split, inner, :].astype(F32)
                q_total = q_total + jnp.sum(jnp.exp(short), axis=-1, keepdims=True)
            stat_col[at, :] = jnp.where(lane == 0, top, jnp.where(lane == 1, total, q_total))
            return carry

        lax.fori_loop(0, groups, step, 0, unroll=2)
        flat = stat_col[pl.ds(pl.multiple_of(z * tokens, tokens), tokens), :].T
        for i in range(3):
            sx_src[:, pl.ds(pl.multiple_of(i * CHUNKS * LANES + z * LANES, LANES), LANES)] = flat[i : i + 1, :]

    def exchange_second(chunk):
        wait_all(buf1[chunk], p1_recv.at[chunk])

        def pick(j, carry):
            source = partner[lax.rem(me_c + j, copies)]
            stage2[chunk, j] = buf1[chunk][lax.rem(me_c - source + copies, copies)]
            return carry

        lax.fori_loop(0, copies, pick, 0)
        to_all("copy", lambda peer, k: stage2.at[chunk, k], buf2.at[chunk], p2_send.at[chunk], p2_recv.at[chunk])
        buf2[chunk, 0] = stage2[chunk, 0]

    wide = CHUNKS * LANES

    def joined(parts):
        tops = parts[:, :, 0:wide]
        top = jnp.max(tops, axis=0)
        factor = jnp.exp(tops - top[None])
        total = jnp.sum(parts[:, :, wide : 2 * wide] * factor, axis=0)
        q_total = jnp.sum(parts[:, :, 2 * wide : 3 * wide] * factor, axis=0)
        return top, total, q_total

    def statistics_x():
        sx_buf[0] = sx_src[...]
        to_all("x", lambda peer, k: sx_src, sx_buf, sx_send.at[0], sx_recv.at[0])

    def statistics_z():
        wait_all(sx_buf, sx_recv.at[0])
        for i, value in enumerate(joined(sx_buf[...])):
            sz_src[:, i * wide : (i + 1) * wide] = value
        sz_buf[0] = sz_src[...]
        to_all("z", lambda peer, k: sz_src, sz_buf, sz_send.at[0], sz_recv.at[0])

    def statistics_copy():
        wait_all(sz_buf, sz_recv.at[0])
        top, total, q_total = joined(sz_buf[...])
        log_total = jnp.log(total)
        cq_src[:, 0:wide] = (sx_src[:, 0:wide] - top) - log_total
        cq_src[:, wide : 2 * wide] = q_total / total
        cq_buf[0] = cq_src[...]
        to_all("copy", lambda peer, k: cq_src, cq_buf, cq_send.at[0], cq_recv.at[0])
        wait_all(sz_buf, sz_send.at[0])
        sz_src[:, 0:wide] = top
        sz_src[:, wide : 2 * wide] = log_total

    def statistics_end():
        wait_all(cq_buf, cq_recv.at[0])
        theirs = cq_buf[lax.rem(me_c - partner[me_c] + copies, copies)]
        for z in range(CHUNKS):
            at = slice(z * LANES, (z + 1) * LANES)
            turned[0:1, :] = sz_src[:, z * LANES : (z + 1) * LANES]
            turned[1:2, :] = sz_src[:, wide + z * LANES : wide + (z + 1) * LANES]
            turned[2:3, :] = theirs[:, z * LANES : (z + 1) * LANES]
            turned[3:4, :] = theirs[:, wide + z * LANES : wide + (z + 1) * LANES]
            stat_col[at, :] = turned[...].T

    def backward(chunk):
        wait_all(buf2.at[chunk], p2_recv.at[chunk])
        z = chunk_z(chunk)
        base = me_f * vocab

        def step(g, carry):
            at = rows_of(z, g)
            here = pl.ds(pl.multiple_of(g * ROWS, ROWS), ROWS)
            token = pl.ds(
                pl.multiple_of((g * ROWS) // share * tokens + z * share + lax.rem(g * ROWS, share), ROWS), ROWS
            )
            first, inner = place(g)
            top, log_total = stat_col[at, 0:1], stat_col[at, 1:2]
            lack, q_total = stat_col[at, 2:3], stat_col[at, 3:4]
            target = t_col[token, 0:1]
            loss = jnp.zeros((ROWS, 1), F32)
            for split in range(splits):
                cols = slice(split * piece_cols, (split + 1) * piece_cols)
                slot = lax.rem(me_c - (first + split) + copies, copies)
                logq = buf2[chunk, slot, inner, :].astype(F32) + lack
                q = jnp.exp(logq)
                value = (logits[at, cols] - top) - log_total
                prob = jnp.exp(value)
                ids = base + split * piece_cols + lax.broadcasted_iota(jnp.int32, (ROWS, piece_cols), 1)
                hot = ids == target
                term = WEIGHT * (q * (logq - value)) - jnp.where(hot, value, 0.0)
                loss = loss + jnp.sum(term, axis=-1, keepdims=True)
                slope = prob - jnp.where(hot, 1.0, 0.0) + WEIGHT * (q_total * prob - q)
                dlog[here, cols] = slope.astype(BF16)
            loss_col[token, :] = jnp.broadcast_to(loss, (ROWS, LANES))
            return carry

        lax.fori_loop(0, groups, step, 0, unroll=2)
        rows = pl.ds(pl.multiple_of(z * tokens, tokens), tokens)

        def product(b, carry):
            at = pl.ds(pl.multiple_of(b * BLOCK, BLOCK), BLOCK)
            piece = lax.dot_general(dlog[...], w[at, :], (((1,), (1,)), ((), ())), preferred_element_type=F32)
            part = jnp.sum(xhat[rows, at] * piece, axis=0, keepdims=True)
            if chunk == 0:
                gacc[:, at] = part
            else:
                gacc[:, at] = gacc[:, at] + part
            return carry

        lax.fori_loop(0, depth // BLOCK, product, 0)

    z_copy(0, 0).start()
    z_copy(1, 0).start()
    spread(0, 0)
    spread(1, 0)
    z_copy(0, 1).start()
    z_copy(1, 1).start()
    pass_on(0)
    loads[3].wait()
    loads[4].wait()
    gather_end(0)
    forward(0)
    z_copy(0, 0).wait_recv()
    z_copy(0, 2).start()
    spread(0, 1)
    z_copy(1, 0).wait_recv()
    z_copy(1, 2).start()
    spread(1, 2)
    z_copy(1, 1).wait_recv()
    spread(1, 1)
    z_copy(0, 1).wait_recv()
    spread(0, 2)
    sums(0)
    pass_on(1)
    pass_on(2)
    gather_end(1)
    forward(1)
    z_copy(0, 2).wait_recv()
    spread(0, 3)
    z_copy(1, 2).wait_recv()
    spread(1, 3)
    gather_end(2)
    forward(2)
    pass_on(3)
    exchange_second(0)
    gather_end(3)
    forward(3)
    for chunk in range(1, CHUNKS):
        sums(chunk)
    statistics_x()
    exchange_second(1)
    statistics_z()
    exchange_second(2)
    statistics_copy()
    exchange_second(3)
    statistics_end()
    for chunk in range(CHUNKS):
        backward(chunk)

    per_row = LANES // share
    for part in range(shards // per_row):
        row = loss_col[part * LANES : (part + 1) * LANES, :].T[0:1, :]
        for j in range(part * per_row, (part + 1) * per_row):
            fin_src[j, :, 0:LANES] = gacc[:, j * LANES : (j + 1) * LANES]
            fin_src[j, :, LANES : 2 * LANES] = row
    to_all("fsdp", lambda peer, k: fin_src.at[peer], fin_buf, f_send.at[0], f_recv.at[0])
    fin_buf[0] = fin_src[me_f]

    for half in (0, 1):
        for slot in range(3):
            z_copy(half, slot).wait_send()
            for chunk in range(CHUNKS):
                x_copy(half, chunk, slot).wait_send()
    for chunk in range(CHUNKS):
        wait_all(buf1[chunk], p1_send.at[chunk])
        wait_all(buf2.at[chunk], p2_send.at[chunk])
    wait_all(sx_buf, sx_send.at[0])
    wait_all(cq_buf, cq_send.at[0])
    wait_all(fin_buf, f_send.at[0])

    wait_all(fin_buf, f_recv.at[0])
    whole = jnp.sum(fin_buf[...], axis=0)
    gg_out[...] = whole[:, 0:LANES]
    row = whole[:, LANES : 2 * LANES]
    result = row[:, 0:share]
    for k in range(1, per_row):
        result = jnp.where(lax.rem(me_f, per_row) == k, row[:, k * share : (k + 1) * share], result)
    tl_out[...] = result


def per_device(copies, shards, hidden, gain, head_weight, targets, partner):
    share, depth = hidden.shape[1], hidden.shape[2]
    vocab = head_weight.shape[2]
    tokens = share * shards
    chunk = share * RING
    groups = min(chunk // ROWS, copies)
    piece = (chunk // groups, vocab // (copies // groups))
    anywhere, vmem = pl.BlockSpec(memory_space=pl.ANY), pl.BlockSpec(memory_space=pltpu.VMEM)
    dma = pltpu.SemaphoreType.DMA
    return pl.pallas_call(
        functools.partial(kernel, copies, shards),
        out_shape=(
            jax.ShapeDtypeStruct((1, depth // shards), F32),
            jax.ShapeDtypeStruct((1, share), F32),
        ),
        in_specs=[anywhere] * 5,
        out_specs=(vmem, vmem),
        scratch_shapes=[
            pltpu.VMEM((depth, vocab), BF16),
            pltpu.VMEM((shards, share, depth), BF16),
            pltpu.VMEM((1, depth), F32),
            pltpu.VMEM((tokens // LANES, LANES), jnp.int32),
            pltpu.SMEM((copies,), jnp.int32),
            pltpu.VMEM((tokens, depth), F32),
            pltpu.VMEM((tokens, depth), BF16),
            pltpu.VMEM((tokens, vocab), F32),
            pltpu.VMEM((chunk, vocab), BF16),
            pltpu.VMEM((tokens, LANES), F32),
            pltpu.VMEM((tokens, LANES), jnp.int32),
            pltpu.VMEM((tokens, LANES), F32),
            pltpu.VMEM((LANES, LANES), F32),
            pltpu.VMEM((1, depth), F32),
            pltpu.VMEM((1, 3 * tokens), F32),
            pltpu.VMEM((RING, 1, 3 * tokens), F32),
            pltpu.VMEM((1, 3 * tokens), F32),
            pltpu.VMEM((RING, 1, 3 * tokens), F32),
            pltpu.VMEM((1, 2 * tokens), F32),
            pltpu.VMEM((copies, 1, 2 * tokens), F32),
            pltpu.VMEM((shards, 1, 2 * LANES), F32),
            pltpu.VMEM((shards, 1, 2 * LANES), F32),
            pltpu.VMEM((CHUNKS, copies) + piece, BF16),
        ]
        + [pltpu.VMEM((copies,) + piece, BF16)] * CHUNKS
        + [pltpu.VMEM((CHUNKS, copies) + piece, BF16)] * 2
        + [
            dma((5,)),
            dma((2 * 3,)),
            dma((2 * 3,)),
            dma((2 * CHUNKS * 3,)),
            dma((2 * CHUNKS * 3,)),
        ]
        + [dma((1,))] * 8
        + [dma((CHUNKS,))] * 4,
        compiler_params=pltpu.CompilerParams(
            collective_id=0, has_side_effects=True, vmem_limit_bytes=56 * 1024 * 1024
        ),
        cost_estimate=pl.CostEstimate(
            flops=4 * tokens * depth * vocab,
            bytes_accessed=2 * depth * vocab,
            transcendentals=4 * tokens * vocab,
        ),
    )(hidden[0], gain, head_weight[0], targets.reshape(-1, LANES), partner)


def solution(mesh):
    in_specs = (P("copy", "fsdp", None), P("copy", None), P("copy", None, "fsdp"), P(), P())
    out_specs = (P("copy", "fsdp"), P("copy", "fsdp"))
    return jax.shard_map(
        functools.partial(per_device, mesh.shape["copy"], mesh.shape["fsdp"]),
        mesh=mesh, in_specs=in_specs, out_specs=out_specs, check_vma=False,
    )
```

time: 442 us -> 113 us (0.26)
  the two profiles are of different devices: /device:TPU:24 before, /device:TPU:1 now
where the time goes in v2:
time: 113 us; the launch traced here: 112 us
  Pallas kernels  110 us (97%)
  local copies, waits for them, and re-layouts  2.25 us (2%)
    pallas_call x1, Pallas kernels, per_device(): pl.pallas_call(functools.partial(kernel, copies, shards), out_shape=(jax....  110 us

profile of v2, /device:TPU:1, one launch (start us, length us, event | category | flops | bytes accessed | tf_op | source)
XLA Modules:
  0.0 112.4 jit_solution(3380201051778613277)
XLA Ops:
  0.6 109.5 %shard_map.68 = (f32[1,128]{1,0:T(1,128)}, f32[1,32]{1,0:T(1,128)}) custom-call(bf16[32,2048]{1,0:T(8,128)(2,1)} %bitcast.4, f32[1,2048]{1,0:T(1,128)} %gain_in.1, bf16[2048,1024]{1,0:T(8,128)(2,1)} %bitcast.3, s32[4,128]{1,0:T(4,128)} %bitcast.5, s32[32]{0:T(128)} %partner_in.1), custom_call_target="tpu_custom_call" | custom-call | flops 4294967296 | bytes 4194304 | tf_op jit(solution)/shard_map/pallas_call | solution.py:401
  110.2 1.1 copy.9
  111.3 1.1 %copy.10 = f32[1,32]{1,0:T(1,128)} copy(f32[1,32]{1,0:T(1,128)} %get-tuple-element.5) | data formatting | bytes 256

commit v3 on v2

--- a/solution.py
+++ b/solution.py
@@ -24,15 +24,16 @@
 
 def kernel(
     copies, shards, hidden_in, gain_in, w_in, targets_in, partner_in, gg_out, tl_out,
-    w, hid, gain, targets, partner, xhat, normed, logits, dlog, stat_col, t_col, loss_col, turned, gacc,
-    sx_src, sx_buf, sz_src, sz_buf, cq_src, cq_buf, fin_src, fin_buf,
+    w, turned_w, hid, gain, targets, partner, xhat, normed, logits, dlog, stat_col, t_col, loss_col, turned, gacc,
+    sx_src, sx_buf, sz_src, sz_buf, qs_row, cq_src, cq_line, cq_plane, fin_src, fin_buf,
     stage1, buf1_0, buf1_1, buf1_2, buf1_3, stage2, buf2,
-    in_sem, z_send, z_recv, x_send, x_recv, sx_send, sx_recv, sz_send, sz_recv, cq_send, cq_recv, f_send, f_recv,
+    in_sem, z_send, z_recv, x_send, x_recv, sx_send, sx_recv, sz_send, sz_recv, cl_send, cl_recv, cp_send, cp_recv, f_send, f_recv,
     p1_send, p1_recv, p2_send, p2_recv,
 ):
     buf1 = (buf1_0, buf1_1, buf1_2, buf1_3)
     me_c, me_f = lax.axis_index("copy"), lax.axis_index("fsdp")
     me_x, me_z = me_f // RING, lax.rem(me_f, RING)
+    line, plane = cq_line.shape[0], cq_plane.shape[0]
     depth, vocab = w.shape
     share = hid.shape[1]
     half_share = share // 2
@@ -61,14 +62,8 @@
 
     lax.fori_loop(1, shards, greet_shard, 0)
     lax.fori_loop(1, copies, greet_copy, 0)
-    sx_src[...] = jnp.zeros_like(sx_src)
-    fin_src[...] = jnp.zeros_like(fin_src)
-    turned[...] = jnp.zeros_like(turned)
-    for load in loads[:3]:
-        load.wait()
-    for part in range(CHUNKS * tokens // LANES):
-        t_col[part * LANES : (part + 1) * LANES, :] = column_of(targets[part : part + 1, :])
     pl.semaphore_wait(barrier, copies + shards - 2)
+    loads[0].wait()
 
     def shard_of(dx, dz):
         return lax.rem(me_x + dx + RING, RING) * RING + lax.rem(me_z + dz + RING, RING)
@@ -107,6 +102,14 @@
         for half in (0, 1):
             x_copy(half, chunk, 1).wait_recv()
             x_copy(half, chunk, 2).wait_recv()
+
+    def place_of(copy):
+        return copy // (2 * line) * 2 + lax.rem(copy, 2), lax.rem(copy // 2, line)
+
+    def copy_at(spot, z):
+        return spot // 2 * (2 * line) + z * 2 + lax.rem(spot, 2)
+
+    mine = place_of(me_c)
 
     def to_all(axis, src_of, buf, send, recv):
         size = buf.shape[0]
@@ -118,6 +121,12 @@
             elif axis == "fsdp":
                 peer = lax.rem(me_f + k, size)
                 device = (me_c, peer)
+            elif axis == "line":
+                peer = copy_at(mine[0], lax.rem(mine[1] + k, line))
+                device = (peer, me_f)
+            elif axis == "plane":
+                peer = copy_at(lax.rem(mine[0] + k, plane), mine[1])
+                device = (peer, me_f)
             elif axis == "x":
                 peer = shard_of(k, 0)
                 device = (me_c, peer)
@@ -133,27 +142,35 @@
         lax.fori_loop(1, size, step, 0)
 
     def wait_all(buf, sem):
-        rest = buf.at[pl.ds(1, buf.shape[0] - 1)]
-        pltpu.make_async_copy(rest, rest, sem).wait()
+        if buf.shape[0] > 1:
+            rest = buf.at[pl.ds(1, buf.shape[0] - 1)]
+            pltpu.make_async_copy(rest, rest, sem).wait()
 
     def chunk_z(chunk):
         return lax.rem(me_z + CHUNK_Z[chunk] + RING, RING)
 
-    def rows_of(z, g):
-        return pl.ds(pl.multiple_of(z * tokens + g * ROWS, ROWS), ROWS)
+    def rows_of(chunk, g):
+        return pl.ds(pl.multiple_of(chunk * tokens + g * ROWS, ROWS), ROWS)
+
+    def rows(chunk, count=1):
+        return slice(chunk * tokens, (chunk + count) * tokens)
+
+    def lanes_of(part, chunk):
+        return pl.ds(pl.multiple_of(part * wide + chunk_z(chunk) * LANES, LANES), LANES)
 
     def place(g):
         first = (g * ROWS) // piece_rows * splits
         return first, pl.ds(pl.multiple_of(lax.rem(g * ROWS, piece_rows), ROWS), ROWS)
 
     groups = tokens // ROWS
+    wide = CHUNKS * LANES
     lane = lax.broadcasted_iota(jnp.int32, (ROWS, LANES), 1)
 
     def forward(chunk):
         z = chunk_z(chunk)
 
         def normalise(g, carry):
-            at = rows_of(z, g)
+            at = rows_of(chunk, g)
             inside = pl.ds(pl.multiple_of(lax.rem(g * ROWS, share), ROWS), ROWS)
             value = hid[(g * ROWS) // share * RING + z, inside, :].astype(F32)
             scale = lax.rsqrt(jnp.mean(value * value, axis=-1, keepdims=True) + OFFSET)
@@ -163,17 +180,16 @@
             return carry
 
         lax.fori_loop(0, groups, normalise, 0, unroll=2)
-        rows = pl.ds(pl.multiple_of(z * tokens, tokens), tokens)
 
         def product(b, carry):
             cols = pl.ds(pl.multiple_of(b * BLOCK, BLOCK), BLOCK)
-            logits[rows, cols] = jnp.dot(normed[rows, :], w[:, cols], preferred_element_type=F32)
+            logits[rows(chunk), cols] = jnp.dot(normed[rows(chunk), :], w[:, cols], preferred_element_type=F32)
             return carry
 
         lax.fori_loop(0, vocab // BLOCK, product, 0)
 
         def rounded(g, carry):
-            at = rows_of(z, g)
+            at = rows_of(chunk, g)
             value = logits[at, :]
             top = jnp.max(value, axis=-1, keepdims=True)
             stat_col[at, :] = jnp.broadcast_to(top, (ROWS, LANES))
@@ -184,14 +200,14 @@
             return carry
 
         lax.fori_loop(0, groups, rounded, 0, unroll=2)
+
+    def exchange_first(chunk):
         to_all("copy", lambda peer, k: stage1.at[chunk, peer], buf1[chunk], p1_send.at[chunk], p1_recv.at[chunk])
         buf1[chunk][0] = stage1[chunk, me_c]
 
     def sums(chunk):
-        z = chunk_z(chunk)
-
         def step(g, carry):
-            at = rows_of(z, g)
+            at = rows_of(chunk, g)
             top = stat_col[at, :]
             total = jnp.sum(jnp.exp(logits[at, :] - top[:, 0:1]), axis=-1, keepdims=True)
             first, inner = place(g)
@@ -203,9 +219,9 @@
             return carry
 
         lax.fori_loop(0, groups, step, 0, unroll=2)
-        flat = stat_col[pl.ds(pl.multiple_of(z * tokens, tokens), tokens), :].T
+        flat = stat_col[rows(chunk), :].T
         for i in range(3):
-            sx_src[:, pl.ds(pl.multiple_of(i * CHUNKS * LANES + z * LANES, LANES), LANES)] = flat[i : i + 1, :]
+            sx_src[:, lanes_of(i, chunk)] = flat[i : i + 1, :]
 
     def exchange_second(chunk):
         wait_all(buf1[chunk], p1_recv.at[chunk])
@@ -218,8 +234,6 @@
         lax.fori_loop(0, copies, pick, 0)
         to_all("copy", lambda peer, k: stage2.at[chunk, k], buf2.at[chunk], p2_send.at[chunk], p2_recv.at[chunk])
         buf2[chunk, 0] = stage2[chunk, 0]
-
-    wide = CHUNKS * LANES
 
     def joined(parts):
         tops = parts[:, :, 0:wide]
@@ -246,31 +260,35 @@
         log_total = jnp.log(total)
         cq_src[:, 0:wide] = (sx_src[:, 0:wide] - top) - log_total
         cq_src[:, wide : 2 * wide] = q_total / total
-        cq_buf[0] = cq_src[...]
-        to_all("copy", lambda peer, k: cq_src, cq_buf, cq_send.at[0], cq_recv.at[0])
+        cq_line[0] = cq_src[...]
+        to_all("line", lambda peer, k: cq_src, cq_line, cl_send.at[0], cl_recv.at[0])
         wait_all(sz_buf, sz_send.at[0])
         sz_src[:, 0:wide] = top
         sz_src[:, wide : 2 * wide] = log_total
 
+    def statistics_plane():
+        wait_all(cq_line, cl_recv.at[0])
+        cq_plane[0] = cq_line[...]
+        to_all("plane", lambda peer, k: cq_line, cq_plane, cp_send.at[0], cp_recv.at[0])
+
     def statistics_end():
-        wait_all(cq_buf, cq_recv.at[0])
-        theirs = cq_buf[lax.rem(me_c - partner[me_c] + copies, copies)]
-        for z in range(CHUNKS):
-            at = slice(z * LANES, (z + 1) * LANES)
-            turned[0:1, :] = sz_src[:, z * LANES : (z + 1) * LANES]
-            turned[1:2, :] = sz_src[:, wide + z * LANES : wide + (z + 1) * LANES]
-            turned[2:3, :] = theirs[:, z * LANES : (z + 1) * LANES]
-            turned[3:4, :] = theirs[:, wide + z * LANES : wide + (z + 1) * LANES]
-            stat_col[at, :] = turned[...].T
-
-    def backward(chunk):
+        wait_all(cq_plane, cp_recv.at[0])
+        spot, z = place_of(partner[me_c])
+        qs_row[...] = cq_plane[lax.rem(mine[0] - spot + plane, plane), lax.rem(mine[1] - z + line, line)]
+        for chunk in range(CHUNKS):
+            turned[0:1, :] = sz_src[:, lanes_of(0, chunk)]
+            turned[1:2, :] = sz_src[:, lanes_of(1, chunk)]
+            turned[2:3, :] = qs_row[:, lanes_of(0, chunk)]
+            turned[3:4, :] = qs_row[:, lanes_of(1, chunk)]
+            stat_col[rows(chunk), :] = turned[...].T
+
+    def slopes(chunk):
         wait_all(buf2.at[chunk], p2_recv.at[chunk])
         z = chunk_z(chunk)
         base = me_f * vocab
 
         def step(g, carry):
-            at = rows_of(z, g)
-            here = pl.ds(pl.multiple_of(g * ROWS, ROWS), ROWS)
+            at = rows_of(chunk, g)
             token = pl.ds(
                 pl.multiple_of((g * ROWS) // share * tokens + z * share + lax.rem(g * ROWS, share), ROWS), ROWS
             )
@@ -291,17 +309,25 @@
                 term = WEIGHT * (q * (logq - value)) - jnp.where(hot, value, 0.0)
                 loss = loss + jnp.sum(term, axis=-1, keepdims=True)
                 slope = prob - jnp.where(hot, 1.0, 0.0) + WEIGHT * (q_total * prob - q)
-                dlog[here, cols] = slope.astype(BF16)
+                dlog[at, cols] = slope.astype(BF16)
             loss_col[token, :] = jnp.broadcast_to(loss, (ROWS, LANES))
             return carry
 
         lax.fori_loop(0, groups, step, 0, unroll=2)
-        rows = pl.ds(pl.multiple_of(z * tokens, tokens), tokens)
-
+
+    def turn_weights():
+        def step(b, carry):
+            at = pl.ds(pl.multiple_of(b * BLOCK, BLOCK), BLOCK)
+            turned_w[:, at] = w[at, :].T
+            return carry
+
+        lax.fori_loop(0, depth // BLOCK, step, 0)
+
+    def gradient(chunk, count):
         def product(b, carry):
             at = pl.ds(pl.multiple_of(b * BLOCK, BLOCK), BLOCK)
-            piece = lax.dot_general(dlog[...], w[at, :], (((1,), (1,)), ((), ())), preferred_element_type=F32)
-            part = jnp.sum(xhat[rows, at] * piece, axis=0, keepdims=True)
+            piece = jnp.dot(dlog[rows(chunk, count), :], turned_w[:, at], preferred_element_type=F32)
+            part = jnp.sum(xhat[rows(chunk, count), at] * piece, axis=0, keepdims=True)
             if chunk == 0:
                 gacc[:, at] = part
             else:
@@ -310,32 +336,44 @@
 
         lax.fori_loop(0, depth // BLOCK, product, 0)
 
+    def prepare():
+        fin_src[...] = jnp.zeros_like(fin_src)
+        turned[...] = jnp.zeros_like(turned)
+        loads[2].wait()
+        for part in range(CHUNKS * tokens // LANES):
+            t_col[part * LANES : (part + 1) * LANES, :] = column_of(targets[part : part + 1, :])
+
+    spread(0, 0)
+    spread(1, 0)
     z_copy(0, 0).start()
     z_copy(1, 0).start()
-    spread(0, 0)
-    spread(1, 0)
     z_copy(0, 1).start()
     z_copy(1, 1).start()
+    prepare()
+    loads[1].wait()
+    loads[3].wait()
     pass_on(0)
-    loads[3].wait()
     loads[4].wait()
+    turn_weights()
     gather_end(0)
     forward(0)
+    exchange_first(0)
     z_copy(0, 0).wait_recv()
     z_copy(0, 2).start()
     spread(0, 1)
     z_copy(1, 0).wait_recv()
     z_copy(1, 2).start()
     spread(1, 2)
+    sums(0)
     z_copy(1, 1).wait_recv()
     spread(1, 1)
     z_copy(0, 1).wait_recv()
     spread(0, 2)
-    sums(0)
     pass_on(1)
     pass_on(2)
     gather_end(1)
     forward(1)
+    exchange_first(1)
     z_copy(0, 2).wait_recv()
     spread(0, 3)
     z_copy(1, 2).wait_recv()
@@ -343,20 +381,28 @@
     gather_end(2)
     forward(2)
     pass_on(3)
+    exchange_first(2)
+    sums(1)
+    sums(2)
     exchange_second(0)
     gather_end(3)
     forward(3)
-    for chunk in range(1, CHUNKS):
-        sums(chunk)
+    sums(3)
     statistics_x()
+    statistics_z()
+    exchange_first(3)
+    statistics_copy()
     exchange_second(1)
-    statistics_z()
+    statistics_plane()
     exchange_second(2)
-    statistics_copy()
     exchange_second(3)
     statistics_end()
-    for chunk in range(CHUNKS):
-        backward(chunk)
+    slopes(0)
+    slopes(1)
+    gradient(0, 2)
+    slopes(2)
+    slopes(3)
+    gradient(2, 2)
 
     per_row = LANES // share
     for part in range(shards // per_row):
@@ -376,7 +422,8 @@
         wait_all(buf1[chunk], p1_send.at[chunk])
         wait_all(buf2.at[chunk], p2_send.at[chunk])
     wait_all(sx_buf, sx_send.at[0])
-    wait_all(cq_buf, cq_send.at[0])
+    wait_all(cq_line, cl_send.at[0])
+    wait_all(cq_plane, cp_send.at[0])
     wait_all(fin_buf, f_send.at[0])
 
     wait_all(fin_buf, f_recv.at[0])
@@ -396,6 +443,7 @@
     chunk = share * RING
     groups = min(chunk // ROWS, copies)
     piece = (chunk // groups, vocab // (copies // groups))
+    line = max(1, copies // 8)
     anywhere, vmem = pl.BlockSpec(memory_space=pl.ANY), pl.BlockSpec(memory_space=pltpu.VMEM)
     dma = pltpu.SemaphoreType.DMA
     return pl.pallas_call(
@@ -408,6 +456,7 @@
         out_specs=(vmem, vmem),
         scratch_shapes=[
             pltpu.VMEM((depth, vocab), BF16),
+            pltpu.VMEM((vocab, depth), BF16),
             pltpu.VMEM((shards, share, depth), BF16),
             pltpu.VMEM((1, depth), F32),
             pltpu.VMEM((tokens // LANES, LANES), jnp.int32),
@@ -415,7 +464,7 @@
             pltpu.VMEM((tokens, depth), F32),
             pltpu.VMEM((tokens, depth), BF16),
             pltpu.VMEM((tokens, vocab), F32),
-            pltpu.VMEM((chunk, vocab), BF16),
+            pltpu.VMEM((tokens, vocab), BF16),
             pltpu.VMEM((tokens, LANES), F32),
             pltpu.VMEM((tokens, LANES), jnp.int32),
             pltpu.VMEM((tokens, LANES), F32),
@@ -426,7 +475,9 @@
             pltpu.VMEM((1, 3 * tokens), F32),
             pltpu.VMEM((RING, 1, 3 * tokens), F32),
             pltpu.VMEM((1, 2 * tokens), F32),
-            pltpu.VMEM((copies, 1, 2 * tokens), F32),
+            pltpu.VMEM((1, 2 * tokens), F32),
+            pltpu.VMEM((line, 1, 2 * tokens), F32),
+            pltpu.VMEM((copies // line, line, 1, 2 * tokens), F32),
             pltpu.VMEM((shards, 1, 2 * LANES), F32),
             pltpu.VMEM((shards, 1, 2 * LANES), F32),
             pltpu.VMEM((CHUNKS, copies) + piece, BF16),
@@ -440,7 +491,7 @@
             dma((2 * CHUNKS * 3,)),
             dma((2 * CHUNKS * 3,)),
         ]
-        + [dma((1,))] * 8
+        + [dma((1,))] * 10
         + [dma((CHUNKS,))] * 4,
         compiler_params=pltpu.CompilerParams(
             collective_id=0, has_side_effects=True, vmem_limit_bytes=56 * 1024 * 1024

time: 113 us -> 102 us (0.903)
  Pallas kernels: 110 us -> 99 us
    pallas_call x1, Pallas kernels: 110 us -> 99 us  [per_device(): pl.pallas_call(functools.partial(kernel, copies, shards), out_shape=(jax....]
where the time goes in v3:
time: 102 us
  Pallas kernels  99 us (97%)
  local copies, waits for them, and re-layouts  2.25 us (2%)
    pallas_call x1, Pallas kernels, per_device(): pl.pallas_call(functools.partial(kernel, copies, shards), out_shape=(jax....  99 us
    unnamed x2, local copies, waits for them, and re-layouts  2.25 us

profile of v3, /device:TPU:1, one launch (start us, length us, event | category | flops | bytes accessed | tf_op | source)
XLA Modules:
  0.0 101.9 jit_solution(14972611628647868407)
XLA Ops:
  0.6 99.0 %shard_map.68 = (f32[1,128]{1,0:T(1,128)}, f32[1,32]{1,0:T(1,128)}) custom-call(bf16[32,2048]{1,0:T(8,128)(2,1)} %bitcast.4, f32[1,2048]{1,0:T(1,128)} %gain_in.1, bf16[2048,1024]{1,0:T(8,128)(2,1)} %bitcast.3, s32[4,128]{1,0:T(4,128)} %bitcast.5, s32[32]{0:T(128)} %partner_in.1), custom_call_target="tpu_custom_call" | custom-call | flops 4294967296 | bytes 4194304 | tf_op jit(solution)/shard_map/pallas_call | solution.py:449
  99.6 1.1 %copy.9 = f32[1,128]{1,0:T(1,128)} copy(f32[1,128]{1,0:T(1,128)} %get-tuple-element.4) | data formatting | bytes 1024
  100.7 1.1 %copy.10 = f32[1,32]{1,0:T(1,128)} copy(f32[1,32]{1,0:T(1,128)} %get-tuple-element.5) | data formatting | bytes 256

commit v4 on v3

--- a/solution.py
+++ b/solution.py
@@ -50,23 +50,21 @@
     for load in loads:
         load.start()
 
+    def shard_of(dx, dz):
+        return lax.rem(me_x + dx + RING, RING) * RING + lax.rem(me_z + dz + RING, RING)
+
     barrier = pltpu.get_barrier_semaphore()
 
     def greet_copy(k, carry):
         pl.semaphore_signal(barrier, inc=1, device_id=(lax.rem(me_c + k, copies), me_f), device_id_type=MESH)
         return carry
 
-    def greet_shard(k, carry):
-        pl.semaphore_signal(barrier, inc=1, device_id=(me_c, lax.rem(me_f + k, shards)), device_id_type=MESH)
-        return carry
-
-    lax.fori_loop(1, shards, greet_shard, 0)
+    for k in range(1, RING):
+        for peer in (shard_of(k, 0), shard_of(0, k)):
+            pl.semaphore_signal(barrier, inc=1, device_id=(me_c, peer), device_id_type=MESH)
     lax.fori_loop(1, copies, greet_copy, 0)
-    pl.semaphore_wait(barrier, copies + shards - 2)
+    pl.semaphore_wait(barrier, copies - 1 + 2 * (RING - 1))
     loads[0].wait()
-
-    def shard_of(dx, dz):
-        return lax.rem(me_x + dx + RING, RING) * RING + lax.rem(me_z + dz + RING, RING)
 
     def hop(which, half, to, send, recv):
         rows = pl.ds(half * half_share, half_share)
@@ -310,7 +308,7 @@
                 loss = loss + jnp.sum(term, axis=-1, keepdims=True)
                 slope = prob - jnp.where(hot, 1.0, 0.0) + WEIGHT * (q_total * prob - q)
                 dlog[at, cols] = slope.astype(BF16)
-            loss_col[token, :] = jnp.broadcast_to(loss, (ROWS, LANES))
+            loss_col[at, :] = jnp.broadcast_to(loss, (ROWS, LANES))
             return carry
 
         lax.fori_loop(0, groups, step, 0, unroll=2)
@@ -322,6 +320,11 @@
             return carry
 
         lax.fori_loop(0, depth // BLOCK, step, 0)
+
+    def losses(chunk):
+        row = loss_col[rows(chunk), :].T[0:1, :]
+        for x in range(RING):
+            fin_src[x * RING + chunk_z(chunk), :, LANES : 2 * LANES] = row
 
     def gradient(chunk, count):
         def product(b, carry):
@@ -400,16 +403,16 @@
     slopes(0)
     slopes(1)
     gradient(0, 2)
+    losses(0)
+    losses(1)
     slopes(2)
     slopes(3)
     gradient(2, 2)
 
-    per_row = LANES // share
-    for part in range(shards // per_row):
-        row = loss_col[part * LANES : (part + 1) * LANES, :].T[0:1, :]
-        for j in range(part * per_row, (part + 1) * per_row):
-            fin_src[j, :, 0:LANES] = gacc[:, j * LANES : (j + 1) * LANES]
-            fin_src[j, :, LANES : 2 * LANES] = row
+    for j in range(shards):
+        fin_src[j, :, 0:LANES] = gacc[:, j * LANES : (j + 1) * LANES]
+    losses(2)
+    losses(3)
     to_all("fsdp", lambda peer, k: fin_src.at[peer], fin_buf, f_send.at[0], f_recv.at[0])
     fin_buf[0] = fin_src[me_f]
 
@@ -424,15 +427,15 @@
     wait_all(sx_buf, sx_send.at[0])
     wait_all(cq_line, cl_send.at[0])
     wait_all(cq_plane, cp_send.at[0])
+
     wait_all(fin_buf, f_send.at[0])
-
     wait_all(fin_buf, f_recv.at[0])
     whole = jnp.sum(fin_buf[...], axis=0)
     gg_out[...] = whole[:, 0:LANES]
     row = whole[:, LANES : 2 * LANES]
     result = row[:, 0:share]
-    for k in range(1, per_row):
-        result = jnp.where(lax.rem(me_f, per_row) == k, row[:, k * share : (k + 1) * share], result)
+    for k in range(1, RING):
+        result = jnp.where(me_x == k, row[:, k * share : (k + 1) * share], result)
     tl_out[...] = result
 
 

time: 102 us -> 102 us (level)
  no operation moved by 1% of the time
where the time goes in v4:
time: 102 us; the launch traced here: 101 us
  Pallas kernels  98.5 us (97%)
  local copies, waits for them, and re-layouts  2.25 us (2%)
    pallas_call x1, Pallas kernels, per_device(): pl.pallas_call(functools.partial(kernel, copies, shards), out_shape=(jax....  98.5 us
    unnamed x2, local copies, waits for them, and re-layouts  2.25 us

profile of v4, /device:TPU:1, one launch (start us, length us, event | category | flops | bytes accessed | tf_op | source)
XLA Modules:
  0.0 101.4 jit_solution(15076674555796051944)
XLA Ops:
  0.6 98.5 %shard_map.68 = (f32[1,128]{1,0:T(1,128)}, f32[1,32]{1,0:T(1,128)}) custom-call(bf16[32,2048]{1,0:T(8,128)(2,1)} %bitcast.4, f32[1,2048]{1,0:T(1,128)} %gain_in.1, bf16[2048,1024]{1,0:T(8,128)(2,1)} %bitcast.3, s32[4,128]{1,0:T(4,128)} %bitcast.5, s32[32]{0:T(128)} %partner_in.1), custom_call_target="tpu_custom_call" | custom-call | flops 4294967296 | bytes 4194304 | tf_op jit(solution)/shard_map/pallas_call | solution.py:452
  99.2 1.1 %copy.9 = f32[1,128]{1,0:T(1,128)} copy(f32[1,128]{1,0:T(1,128)} %get-tuple-element.4) | data formatting | bytes 1024
  100.3 1.1 %copy.10 = f32[1,32]{1,0:T(1,128)} copy(f32[1,32]{1,0:T(1,128)} %get-tuple-element.5) | data formatting | bytes 256

commit v5 on v4

--- a/solution.py
+++ b/solution.py
@@ -27,7 +27,7 @@
     w, turned_w, hid, gain, targets, partner, xhat, normed, logits, dlog, stat_col, t_col, loss_col, turned, gacc,
     sx_src, sx_buf, sz_src, sz_buf, qs_row, cq_src, cq_line, cq_plane, fin_src, fin_buf,
     stage1, buf1_0, buf1_1, buf1_2, buf1_3, stage2, buf2,
-    in_sem, z_send, z_recv, x_send, x_recv, sx_send, sx_recv, sz_send, sz_recv, cl_send, cl_recv, cp_send, cp_recv, f_send, f_recv,
+    line_sem, in_sem, z_send, z_recv, x_send, x_recv, sx_send, sx_recv, sz_send, sz_recv, cl_send, cl_recv, cp_send, cp_recv, f_send, f_recv,
     p1_send, p1_recv, p2_send, p2_recv,
 ):
     buf1 = (buf1_0, buf1_1, buf1_2, buf1_3)
@@ -53,17 +53,24 @@
     def shard_of(dx, dz):
         return lax.rem(me_x + dx + RING, RING) * RING + lax.rem(me_z + dz + RING, RING)
 
+    def place_of(copy):
+        return copy // (2 * line) * 2 + lax.rem(copy, 2), lax.rem(copy // 2, line)
+
+    def copy_at(spot, z):
+        return spot // 2 * (2 * line) + z * 2 + lax.rem(spot, 2)
+
+    mine = place_of(me_c)
+
     barrier = pltpu.get_barrier_semaphore()
-
-    def greet_copy(k, carry):
-        pl.semaphore_signal(barrier, inc=1, device_id=(lax.rem(me_c + k, copies), me_f), device_id_type=MESH)
-        return carry
 
     for k in range(1, RING):
         for peer in (shard_of(k, 0), shard_of(0, k)):
             pl.semaphore_signal(barrier, inc=1, device_id=(me_c, peer), device_id_type=MESH)
-    lax.fori_loop(1, copies, greet_copy, 0)
-    pl.semaphore_wait(barrier, copies - 1 + 2 * (RING - 1))
+    plane_peers = [copy_at(lax.rem(mine[0] + k, plane), mine[1]) for k in range(1, plane)]
+    line_peers = [copy_at(mine[0], lax.rem(mine[1] + k, line)) for k in range(1, line)]
+    for peer in line_peers + plane_peers:
+        pl.semaphore_signal(barrier, inc=1, device_id=(peer, me_f), device_id_type=MESH)
+    pl.semaphore_wait(barrier, line + plane - 2 + 2 * (RING - 1))
     loads[0].wait()
 
     def hop(which, half, to, send, recv):
@@ -100,14 +107,6 @@
         for half in (0, 1):
             x_copy(half, chunk, 1).wait_recv()
             x_copy(half, chunk, 2).wait_recv()
-
-    def place_of(copy):
-        return copy // (2 * line) * 2 + lax.rem(copy, 2), lax.rem(copy // 2, line)
-
-    def copy_at(spot, z):
-        return spot // 2 * (2 * line) + z * 2 + lax.rem(spot, 2)
-
-    mine = place_of(me_c)
 
     def to_all(axis, src_of, buf, send, recv):
         size = buf.shape[0]
@@ -352,6 +351,8 @@
     z_copy(1, 0).start()
     z_copy(0, 1).start()
     z_copy(1, 1).start()
+    for peer in plane_peers:
+        pl.semaphore_signal(line_sem, inc=1, device_id=(peer, me_f), device_id_type=MESH)
     prepare()
     loads[1].wait()
     loads[3].wait()
@@ -360,6 +361,7 @@
     turn_weights()
     gather_end(0)
     forward(0)
+    pl.semaphore_wait(line_sem, plane - 1)
     exchange_first(0)
     z_copy(0, 0).wait_recv()
     z_copy(0, 2).start()
@@ -488,6 +490,7 @@
         + [pltpu.VMEM((copies,) + piece, BF16)] * CHUNKS
         + [pltpu.VMEM((CHUNKS, copies) + piece, BF16)] * 2
         + [
+            pltpu.SemaphoreType.REGULAR,
             dma((5,)),
             dma((2 * 3,)),
             dma((2 * 3,)),

time: 102 us -> 101 us (level)
  no operation moved by 1% of the time
where the time goes in v5:
time: 101 us
  Pallas kernels  97.9 us (97%)
  local copies, waits for them, and re-layouts  2.25 us (2%)
    pallas_call x1, Pallas kernels, per_device(): pl.pallas_call(functools.partial(kernel, copies, shards), out_shape=(jax....  97.9 us
    unnamed x2, local copies, waits for them, and re-layouts  2.25 us

profile of v5, /device:TPU:1, one launch (start us, length us, event | category | flops | bytes accessed | tf_op | source)
XLA Modules:
  0.0 100.7 jit_solution(5508738612444681394)
XLA Ops:
  0.6 97.9 %shard_map.68 = (f32[1,128]{1,0:T(1,128)}, f32[1,32]{1,0:T(1,128)}) custom-call(bf16[32,2048]{1,0:T(8,128)(2,1)} %bitcast.4, f32[1,2048]{1,0:T(1,128)} %gain_in.1, bf16[2048,1024]{1,0:T(8,128)(2,1)} %bitcast.3, s32[4,128]{1,0:T(4,128)} %bitcast.5, s32[32]{0:T(128)} %partner_in.1), custom_call_target="tpu_custom_call" | custom-call | flops 4294967296 | bytes 4194304 | tf_op jit(solution)/shard_map/pallas_call | solution.py:454
  98.5 1.1 %copy.9 = f32[1,128]{1,0:T(1,128)} copy(f32[1,128]{1,0:T(1,128)} %get-tuple-element.4) | data formatting | bytes 1024
  99.6 1.1 %copy.10 = f32[1,32]{1,0:T(1,128)} copy(f32[1,32]{1,0:T(1,128)} %get-tuple-element.5) | data formatting | bytes 256
